TPU v7x, 32 devices: a whole 2x2x4 slice. The times are simulated.
32 devices in a mesh: dp: 4 (over y, x), cent: 4 (over z), rep: 2 (over core).
Axes of the slice: x: 2, y: 2, z: 4, core: 2. Of those that a mesh axis runs over, the one named last changes fastest.
Arguments:
- rows: bfloat16 [16384, 1024], P(('dp', 'rep')), may hold values from -15 to 15
- panel: bfloat16 [4096, 1024], P('cent'), may hold values from -2.15 to 2.15
- scales: float32 [4096, 8], P('cent'), may hold values from 0.7 to 1.4
- inv_temp: int32 [1], replicated, may hold values from 4 to 15
Outputs:
- centroid_sums: float32 [1024, 4096], P(('dp', 'rep'), 'cent')
- centroid_counts: float32 [4096], P('cent')
All inputs are finite; a program needn't handle non-finite values.
Results may differ from a plain program's by a relative error of at most 0.04.
Values may be sent and summed in bfloat16 or wider, within the bound.
A program may use at most 64 MiB of HBM per device.

v0:
```python
import math

import jax
import jax.numpy as jnp
from jax import lax
from jax.sharding import PartitionSpec as P


def dequantize(panel, scales):
    count, width = panel.shape
    blocks = scales.shape[1]
    full = panel.astype(jnp.float32).reshape(count, blocks, width // blocks) * scales[:, :, None]
    return full.reshape(count, width).astype(jnp.bfloat16)


def stats_cent(local_max, local_total):
    top = lax.pmax(local_max, "cent")
    total = lax.psum(local_total * jnp.exp(local_max - top), "cent")
    return (top, total)


def local_logits(row_block, centroids, factor):
    norms = jnp.sum(centroids.astype(jnp.float32) ** 2, axis=1)
    prod = lax.dot_general(
        row_block, centroids, (((1,), (1,)), ((), ())), preferred_element_type=jnp.float32
    )
    return (prod - 0.5 * norms[None, :]) * factor


def on_device(rows, panel, scales, inv_temp):
    width = rows.shape[1]
    factor = inv_temp[0].astype(jnp.float32) / math.sqrt(width)
    centroids = dequantize(panel, scales)
    logits = local_logits(rows, centroids, factor)
    local_max = jnp.max(logits, axis=1)
    local_total = jnp.sum(jnp.exp(logits - local_max[:, None]), axis=1)
    top, total = stats_cent(local_max, local_total)
    weights = (jnp.exp(logits - top[:, None]) / total[:, None]).astype(jnp.bfloat16)
    sums = lax.psum_scatter(
        lax.dot_general(
            rows, weights, (((0,), (0,)), ((), ())), preferred_element_type=jnp.float32
        ),
        ("dp", "rep"),
        scatter_dimension=0,
        tiled=True,
    )
    counts = lax.psum(jnp.sum(weights.astype(jnp.float32), axis=0), ("dp", "rep"))
    return (sums, counts)


def solution(mesh):
    in_specs = (P(("dp", "rep"), None), P("cent", None), P("cent", None), P())
    out_specs = (P(("dp", "rep"), "cent"), P("cent"))
    return jax.shard_map(
        on_device, mesh=mesh, in_specs=in_specs, out_specs=out_specs, check_vma=False
    )
```

profile of v0, /device:TPU:0, one launch (start us, length us, event | category | flops | bytes accessed | tf_op | source)
XLA Modules:
  0.0 116.9 jit_solution(13331207734357335430)
XLA Ops:
  7.2 0.0 copy-start
  7.2 0.0 reduce-scatter.2.cloned.1.call-start
  8.0 1.0 copy.6
  9.0 1.1 mul.32
  10.1 0.0 copy-start.1
  10.1 0.0 copy-done
  10.1 0.7 multiply_reduce_fusion
  10.9 1.4 %copy-done.1 = bf16[2048,1024]{1,0:T(8,128)(2,1)S(1)} copy-done((bf16[2048,1024]{1,0:T(8,128)(2,1)S(1)}, bf16[2048,1024]{1,0:T(8,128)(2,1)}, u32[]{:S(2)}) %copy-start.1) | copy-done | bytes 4194328
  12.3 6.9 %fusion = (f32[2048]{0:T(1024)S(1)}, f32[1024,2048]{1,0:T(8,128)}) fusion(f32[]{:T(128)} %bitcast, f32[1024]{0:T(1024)S(1)} %broadcast_multiply_fusion, bf16[2048,1024]{1,0:T(8,128)(2,1)S(1)} %copy-done.1, f32[128,8,8,128]{3,2,1,0:T(8,128)S(1)} %bitcast.17, bf16[1024,1024]{1,0:T(8,128)(2,1)S(1)} %copy-done), kind=kOutput, calls=%fused_computation.4 | convolution fusion | flops 4304402432 | bytes 18886660 | tf_op jit(solution)/shard_map/dot_general | solution.py:24
  19.2 13.7 %pmax.7 = f32[2048]{0:T(1024)S(1)} all-reduce(f32[2048]{0:T(1024)S(1)} %get-tuple-element.6), channel_id=1, replica_groups=mesh['dp'=4,'cent'=4,'rep'=2] {'cent'}, use_global_device_ids=true, to_apply=%region_2.0 | all-reduce | flops 2048 | bytes 16384 | tf_op jit(solution)/shard_map/pmax | solution.py:17
  32.9 4.5 %exponential_reduce_fusion = f32[2048]{0:T(1024)S(1)} fusion(f32[1024,2048]{1,0:T(8,128)} %get-tuple-element.7, f32[2048]{0:T(1024)S(1)} %get-tuple-element.6, f32[]{:T(128)} %bitcast, f32[1024]{0:T(1024)S(1)} %broadcast_multiply_fusion), kind=kLoop, calls=%fused_computation.2 | loop fusion | flops 8386560 | bytes 8409092 | tf_op jit(solution)/shard_map/reduce_sum | solution.py:36
  37.4 8.5 %psum.14 = f32[2048]{0:T(1024)S(1)} all-reduce(f32[2048]{0:T(1024)S(1)} %exponential_multiply_fusion), channel_id=1, replica_groups=mesh['dp'=4,'cent'=4,'rep'=2] {'cent'}, use_global_device_ids=true, to_apply=%region_4.0 | all-reduce | flops 2048 | bytes 16384 | tf_op jit(solution)/shard_map/psum | solution.py:18
  45.9 0.0 copy-start.2
  45.9 4.9 %convert_reduce_fusion = (f32[1024]{0:T(1024)S(1)}, bf16[1024,2048]{1,0:T(8,128)(2,1)S(1)}) fusion(f32[2048]{0:T(1024)S(1)} %psum.14, f32[2048]{0:T(1024)S(1)} %pmax.7, f32[]{:T(128)} %bitcast, f32[1024,2048]{1,0:T(8,128)} %get-tuple-element.7, f32[1024]{0:T(1024)S(1)} %broadcast_multiply_fusion), kind=kLoop, calls=%fused_computation | loop fusion | flops 14679040 | bytes 12607492 | tf_op jit(solution)/shard_map/reduce_sum | solution.py:47
  50.8 0.0 copy-done.2
  50.8 6.0 %convolution_bitcast_fusion = f32[1024,1024]{0,1:T(8,128)} fusion(bf16[1024,2048]{1,0:T(8,128)(2,1)S(1)} %get-tuple-element.5, bf16[2048,1024]{1,0:T(8,128)(2,1)S(1)} %copy-done.2), kind=kOutput, calls=%fused_computation.8 | convolution fusion | flops 4294967296 | bytes 12582912 | tf_op jit(solution)/shard_map/dot_general | solution.py:40
  56.9 0.0 reduce-scatter.2.cloned.1.call-update
  56.9 12.4 %psum.15 = f32[1024]{0:T(1024)} all-reduce(f32[1024]{0:T(1024)S(1)} %get-tuple-element.4), channel_id=1, replica_groups=mesh['dp'=4,'cent'=4,'rep'=2] {'dp','rep'}, use_global_device_ids=true, to_apply=%region_7.0 | all-reduce | flops 1024 | bytes 8192 | tf_op jit(solution)/shard_map/psum | solution.py:47
  69.3 38.7 %reduce-scatter.2.cloned.1.call-done = f32[128,1024]{0,1:T(8,128)} async-done(((f32[1024,1024]{0,1:T(8,128)}), f32[128,1024]{0,1:T(8,128)}) %reduce-scatter.2.cloned.1.call-update) | async-done | bytes 524304 | tf_op jit(solution)/shard_map/reduce_scatter | solution.py:39
  108.0 2.0 %copy.7 = f32[128,1024]{1,0:T(8,128)} copy(f32[128,1024]{0,1:T(8,128)} %reduce-scatter.2.cloned.1.call-done) | data formatting | bytes 1048576
  (2 shorter events, 0.0 us)
Async XLA Ops:
  7.2 3.0 %copy-start = (bf16[1024,1024]{1,0:T(8,128)(2,1)S(1)}, bf16[1024,1024]{1,0:T(8,128)(2,1)}, u32[]{:S(2)}) copy-start(bf16[1024,1024]{1,0:T(8,128)(2,1)} %param.5) | copy-start | bytes 6291460
  7.2 100.8 %reduce-scatter.2.cloned.1.call-start = ((), (), s32[]{:S(2)}) async-start(), calls=%async_computation.1 | async-start | bytes 4718592 | tf_op jit(solution)/shard_map/reduce_scatter | solution.py:39
  10.1 2.2 %copy-start.1 = (bf16[2048,1024]{1,0:T(8,128)(2,1)S(1)}, bf16[2048,1024]{1,0:T(8,128)(2,1)}, u32[]{:S(2)}) copy-start(bf16[2048,1024]{1,0:T(8,128)(2,1)} %param.4) | copy-start | bytes 12582916
  45.9 4.9 %copy-start.2 = (bf16[2048,1024]{1,0:T(8,128)(2,1)S(1)}, bf16[2048,1024]{1,0:T(8,128)(2,1)}, u32[]{:S(2)}) copy-start(bf16[2048,1024]{1,0:T(8,128)(2,1)} %param.4) | copy-start | bytes 12582916
Sparse Core Ops, SparseCore 0:
  57.0 50.9 reduce-scatter.1
where the time goes:
time: 117 us
  waiting for transfers between devices  38.7 us (33%)
  blocking collectives  34.6 us (30%)
  between operations  14.9 us (13%)
  matrix products  12.9 us (11%)
  other arithmetic  10.1 us (9%)
  local copies, waits for them, and re-layouts  5.55 us (5%)
    reduce_scatter x1, waiting for transfers between devices, on_device(): lax.psum_scatter(lax.dot_general(rows, weights, (((0,), (0,)), ((), ())),...  38.7 us
    pmax x1, blocking collectives, stats_cent(): top = lax.pmax(local_max, 'cent')  13.7 us
    psum x1, blocking collectives, on_device(): lax.psum(jnp.sum(weights.astype(jnp.float32), axis=0), ('dp', 'rep'))  12.4 us
    psum x1, blocking collectives, stats_cent(): total = lax.psum(local_total * jnp.exp(local_max - top), 'cent')  8.52 us
    dot_general x1, matrix products, local_logits(): lax.dot_general(row_block, centroids, (((1,), (1,)), ((), ())), preferred...  6.88 us
    dot_general x1, matrix products, on_device(): lax.dot_general(rows, weights, (((0,), (0,)), ((), ())), preferred_elemen...  6.05 us
    reduce_sum x1, other arithmetic, on_device(): jnp.sum(weights.astype(jnp.float32), axis=0)  4.85 us
    reduce_sum x1, other arithmetic, on_device(): local_total = jnp.sum(jnp.exp(logits - local_max[:, None]), axis=1)  4.51 us
  transfers between devices with their start and end apart: 1, of which 1 were waited for; matrix products, arithmetic and copies ran while one was open for 0% of the time, Pallas kernels for 0%

commit v1 on v0

v1 whole, which is shorter than its diff:
```python
import functools
import math

import jax
import jax.numpy as jnp
from jax import lax
from jax.experimental import pallas as pl
from jax.experimental.pallas import tpu as pltpu
from jax.sharding import PartitionSpec as P

MESH = pl.DeviceIdType.MESH
NT = (((1,), (1,)), ((), ()))
NN = (((1,), (0,)), ((), ()))
LANES = 128


def flip(index, mask, bits):
    for b in range(bits):
        if (mask >> b) & 1:
            index = index + (1 << b) - (2 << b) * ((index // (1 << b)) % 2)
    return index


def first_step(q, order):
    for j, b in enumerate(order):
        if (q >> b) & 1:
            return j
    return len(order)


def kernel(dp_n, cent_n, rep_n, parts,
           rows_hbm, panel_hbm, scales_ref, temp_ref,
           out_ref, counts_ref, *scratch):
    n_chunks, tile = parts
    scratch = list(scratch)
    rows_ref, panel_ref, cent_ref, bias_ref, w_ref, cnt_ref = scratch[:6]
    t_refs = scratch[6:6 + n_chunks]
    (own_ref, core_out, core_in, dp_out, dp_in, stat_out, stat_in, cnt_out, cnt_in,
     rows_sem, panel_sem, core_ss, core_rs, dp_ss, dp_rs, stat_ss, stat_rs,
     cnt_ss, cnt_rs) = scratch[6 + n_chunks:]

    n_rows, width = rows_ref.shape
    n_cent = cent_ref.shape[0]
    n = n_rows // n_chunks
    n_blk = scales_ref.shape[1]
    blk = width // n_blk
    fb = out_ref.shape[1]
    half = n_cent // 2
    bits = dp_n.bit_length() - 1

    d = lax.axis_index("dp")
    z = lax.axis_index("cent")
    r = lax.axis_index("rep")

    panel_copy = pltpu.make_async_copy(panel_hbm, panel_ref, panel_sem)
    panel_copy.start()
    row_copies = []
    for c in range(n_chunks):
        cp = pltpu.make_async_copy(
            rows_hbm.at[pl.ds(c * n, n)], rows_ref.at[pl.ds(c * n, n)], rows_sem.at[c])
        cp.start()
        row_copies.append(cp)

    z_peers = [lax.rem(z + o, cent_n) for o in range(1, cent_n)]
    group = [(lax.rem(d + o // rep_n, dp_n), lax.rem(r + o % rep_n, rep_n))
             for o in range(1, dp_n * rep_n)]
    barrier = pltpu.get_barrier_semaphore()
    for peer in z_peers:
        pl.semaphore_signal(barrier, inc=1, device_id={"cent": peer}, device_id_type=MESH)
    for pd, pr in group:
        pl.semaphore_signal(barrier, inc=1, device_id={"dp": pd, "rep": pr}, device_id_type=MESH)

    scale2 = temp_ref[0].astype(jnp.float32) * (math.log2(math.e) / math.sqrt(width))

    panel_copy.wait()
    for k in range(0, n_cent, tile):
        sq = jnp.zeros((tile, blk), jnp.float32)
        for b in range(n_blk):
            full = panel_ref[k:k + tile, b * blk:(b + 1) * blk].astype(jnp.float32)
            full = (full * scales_ref[k:k + tile, b:b + 1]).astype(jnp.bfloat16)
            cent_ref[k:k + tile, b * blk:(b + 1) * blk] = full
            wide = full.astype(jnp.float32)
            sq = sq + wide * wide
        norm = jnp.sum(sq, axis=1, keepdims=True)
        bias_ref[k:k + tile, :] = jnp.broadcast_to((-0.5 * scale2) * norm, (tile, LANES))

    pl.semaphore_wait(barrier, len(z_peers) + len(group))

    stat_copies = []

    def logits_tile(c, k):
        prod = lax.dot_general(cent_ref[k:k + tile, :], rows_ref[c * n:(c + 1) * n, :], NT,
                               preferred_element_type=jnp.float32)
        bias = jnp.concatenate([bias_ref[k:k + tile, :]] * (n // LANES), axis=1)
        t = prod * scale2 + bias
        t_refs[c][k:k + tile, :] = t
        return jnp.max(t.reshape(tile // 8, 8, n), axis=0)

    def exp_tile(c, k, top):
        e = jnp.exp2(t_refs[c][k:k + tile, :] - top)
        t_refs[c][k:k + tile, :] = e
        return jnp.sum(e.reshape(tile // 8, 8, n), axis=0)

    def send_stats(c, top, total):
        stat_out[c, 0:1, :] = top
        stat_out[c, 1:2, :] = total
        for o, peer in enumerate(z_peers):
            cp = pltpu.make_async_remote_copy(
                stat_out.at[c], stat_in.at[c, o], stat_ss.at[c, o], stat_rs.at[c, o],
                device_id={"cent": peer}, device_id_type=MESH)
            cp.start()
            stat_copies.append(cp)

    tops = [None] * n_chunks
    for c in range(n_chunks + 1):
        if c < n_chunks:
            row_copies[c].wait()
        best = total = None
        for k in range(0, n_cent, tile):
            if c < n_chunks:
                m = logits_tile(c, k)
                best = m if best is None else jnp.maximum(best, m)
            if c > 0:
                s = exp_tile(c - 1, k, tops[c - 1])
                total = s if total is None else total + s
        if c < n_chunks:
            tops[c] = jnp.max(best, axis=0, keepdims=True)
        if c > 0:
            send_stats(c - 1, tops[c - 1], jnp.sum(total, axis=0, keepdims=True))

    def weights(c):
        for cp in stat_copies[c * len(z_peers):(c + 1) * len(z_peers)]:
            cp.wait_recv()
        mine = stat_out[c, 0:1, :]
        top = mine
        for o in range(len(z_peers)):
            top = jnp.maximum(top, stat_in[c, o, 0:1, :])
        total = stat_out[c, 1:2, :] * jnp.exp2(mine - top)
        for o in range(len(z_peers)):
            total = total + stat_in[c, o, 1:2, :] * jnp.exp2(stat_in[c, o, 0:1, :] - top)
        ratio = jnp.exp2(mine - top) / total
        for k in range(0, n_cent, tile):
            w = t_refs[c][k:k + tile, :] * ratio
            w_ref[k:k + tile, c * n:(c + 1) * n] = w.astype(jnp.bfloat16)
            part = w[:, :LANES]
            for l in range(LANES, n, LANES):
                part = part + w[:, l:l + LANES]
            if c > 0:
                part = part + cnt_ref[k:k + tile, :]
            cnt_ref[k:k + tile, :] = part

    def columns(q):
        return pl.ds(pl.multiple_of(flip(d, q, bits) * (2 * fb), 2 * fb), 2 * fb)

    core_copies = {}
    dp_copies = {}

    def split(h, q, prod):
        first = r == 0
        own_ref[h, q] = jnp.where(first, prod[:, :fb], prod[:, fb:])
        core_out[h, q] = jnp.where(first, prod[:, fb:], prod[:, :fb]).astype(jnp.bfloat16)
        cp = pltpu.make_async_remote_copy(
            core_out.at[h, q], core_in.at[h, q], core_ss.at[h, q], core_rs.at[h, q],
            device_id={"rep": 1 - r}, device_id_type=MESH)
        cp.start()
        core_copies[h, q] = cp

    orders = [list(range(bits)), list(range(bits))[::-1]]

    def unit(h, q):
        split(h, q, lax.dot_general(w_ref[h * half:(h + 1) * half, :], rows_ref[:, columns(q)], NN,
                                    preferred_element_type=jnp.float32))

    def finish(h, q):
        order = orders[h]
        j = first_step(q, order)
        core_copies[h, q].wait_recv()
        total = own_ref[h, q] + core_in[h, q].astype(jnp.float32)
        for i in range(j):
            src = q ^ (1 << order[i])
            dp_copies[h, src].wait_recv()
            total = total + dp_in[h, src - 1].astype(jnp.float32)
        if q == 0:
            out_ref[h * half:(h + 1) * half, :] = total
            return
        dp_out[h, q - 1] = total.astype(jnp.bfloat16)
        cp = pltpu.make_async_remote_copy(
            dp_out.at[h, q - 1], dp_in.at[h, q - 1], dp_ss.at[h, q - 1], dp_rs.at[h, q - 1],
            device_id={"dp": flip(d, 1 << order[j], bits)}, device_id_type=MESH)
        cp.start()
        dp_copies[h, q] = cp

    ranked = []
    for order in orders:
        ranked.append(sorted(range(dp_n), reverse=True,
                             key=lambda q: [(q >> b) & 1 for b in order]))
    todo = [(h, ranked[h][i]) for i in range(dp_n) for h in range(2)]

    acc = None
    h0, q0 = todo[0]
    for c in range(n_chunks):
        weights(c)
        p = lax.dot_general(w_ref[h0 * half:(h0 + 1) * half, c * n:(c + 1) * n],
                            rows_ref[c * n:(c + 1) * n, columns(q0)], NN,
                            preferred_element_type=jnp.float32)
        acc = p if acc is None else acc + p
    split(h0, q0, acc)

    cnt_out[...] = jnp.sum(cnt_ref[...].T, axis=0, keepdims=True)
    cnt_copies = []
    for o, (pd, pr) in enumerate(group):
        cp = pltpu.make_async_remote_copy(
            cnt_out, cnt_in.at[o], cnt_ss.at[o], cnt_rs.at[o],
            device_id={"dp": pd, "rep": pr}, device_id_type=MESH)
        cp.start()
        cnt_copies.append(cp)

    done = 0
    for i in range(1, len(todo)):
        unit(*todo[i])
        h, q = todo[done]
        if done < i and first_step(q, orders[h]) == 0:
            finish(h, q)
            done += 1
    for h, q in todo[done:-2]:
        finish(h, q)

    counts = cnt_out[...]
    for o, cp in enumerate(cnt_copies):
        cp.wait_recv()
        counts = counts + cnt_in[o]
    counts_ref[...] = counts

    for h, q in todo[-2:]:
        finish(h, q)

    for cp in stat_copies + cnt_copies + list(core_copies.values()) + list(dp_copies.values()):
        cp.wait_send()


def on_device(sizes, rows, panel, scales, inv_temp):
    dp_n, cent_n, rep_n = sizes
    n_rows, width = rows.shape
    n_cent = panel.shape[0]
    n_chunks = 4
    tile = 256
    n = n_rows // n_chunks
    fb = width // (dp_n * rep_n)
    half = n_cent // 2
    group = dp_n * rep_n - 1
    f32, bf16 = jnp.float32, jnp.bfloat16
    dma = pltpu.SemaphoreType.DMA
    body = functools.partial(kernel, dp_n, cent_n, rep_n, (n_chunks, tile))
    sums, counts = pl.pallas_call(
        body,
        out_shape=(jax.ShapeDtypeStruct((n_cent, fb), f32), jax.ShapeDtypeStruct((1, n_cent), f32)),
        in_specs=[pl.BlockSpec(memory_space=pl.ANY), pl.BlockSpec(memory_space=pl.ANY),
                  pl.BlockSpec(memory_space=pltpu.VMEM), pl.BlockSpec(memory_space=pltpu.SMEM)],
        out_specs=(pl.BlockSpec(memory_space=pltpu.VMEM), pl.BlockSpec(memory_space=pltpu.VMEM)),
        scratch_shapes=[
            pltpu.VMEM((n_rows, width), bf16),
            pltpu.VMEM((n_cent, width), bf16),
            pltpu.VMEM((n_cent, width), bf16),
            pltpu.VMEM((n_cent, LANES), f32),
            pltpu.VMEM((n_cent, n_rows), bf16),
            pltpu.VMEM((n_cent, LANES), f32),
            *[pltpu.VMEM((n_cent, n), f32) for _ in range(n_chunks)],
            pltpu.VMEM((2, dp_n, half, fb), f32),
            pltpu.VMEM((2, dp_n, half, fb), bf16),
            pltpu.VMEM((2, dp_n, half, fb), bf16),
            pltpu.VMEM((2, dp_n - 1, half, fb), bf16),
            pltpu.VMEM((2, dp_n - 1, half, fb), bf16),
            pltpu.VMEM((n_chunks, 2, n), f32),
            pltpu.VMEM((n_chunks, cent_n - 1, 2, n), f32),
            pltpu.VMEM((1, n_cent), f32),
            pltpu.VMEM((group, 1, n_cent), f32),
            dma((n_chunks,)), dma,
            dma((2, dp_n)), dma((2, dp_n)),
            dma((2, dp_n - 1)), dma((2, dp_n - 1)),
            dma((n_chunks, cent_n - 1)), dma((n_chunks, cent_n - 1)),
            dma((group,)), dma((group,)),
        ],
        compiler_params=pltpu.CompilerParams(
            collective_id=0, has_side_effects=True, vmem_limit_bytes=56 * 1024 * 1024),
    )(rows, panel, scales, inv_temp)
    return sums.T, counts.reshape(n_cent)


def solution(mesh):
    sizes = (mesh.shape["dp"], mesh.shape["cent"], mesh.shape["rep"])
    in_specs = (P(("dp", "rep"), None), P("cent", None), P("cent", None), P())
    out_specs = (P(("dp", "rep"), "cent"), P("cent"))
    return jax.shard_map(
        functools.partial(on_device, sizes), mesh=mesh, in_specs=in_specs, out_specs=out_specs,
        check_vma=False,
    )
```

time: 117 us -> 40.8 us (0.35)
  waiting for transfers between devices: 38.7 us -> 0 us
  blocking collectives: 34.6 us -> 0 us
  Pallas kernels: 0 us -> 34.1 us
  between operations: 14.9 us -> 1.29 us
  matrix products: 12.9 us -> 0 us
  other arithmetic: 10.1 us -> 0 us
    reduce_scatter x1 -> x0, waiting for transfers between devices: 38.7 us -> none  [on_device(): lax.psum_scatter(lax.dot_general(rows, weights, (((0,), (0,)), ((), ())),...]
    pallas_call x0 -> x1, Pallas kernels: none -> 34.1 us  [on_device(): pl.pallas_call(body, out_shape=(jax.ShapeDtypeStruct((n_cent, fb), f32),...]
    psum x2 -> x0, blocking collectives: 20.9 us -> none  [the longest x1 12.4 us: on_device(): lax.psum(jnp.sum(weights.astype(jnp.float32), axis=0), ('dp', 'rep'))]
    pmax x1 -> x0, blocking collectives: 13.7 us -> none  [stats_cent(): top = lax.pmax(local_max, 'cent')]
    dot_general x2 -> x0, matrix products: 12.9 us -> none  [the longest x1 6.88 us: local_logits(): lax.dot_general(row_block, centroids, (((1,), (1,)), ((), ())), preferred...]
    reduce_sum x3 -> x0, other arithmetic: 10.1 us -> none  [the longest x1 4.85 us: on_device(): jnp.sum(weights.astype(jnp.float32), axis=0)]
    unnamed x8 -> x3, local copies, waits for them, and re-layouts: 4.41 us -> 5.06 us
  transfers between devices with their start and end apart: 1 -> 0, of which waited for: 1 -> 0; matrix products, arithmetic and copies ran while one was open for 0% -> 0% of each run, Pallas kernels for 0% -> 0%
where the time goes in v1:
time: 40.8 us; the launch traced here: 40.4 us
  Pallas kernels  34.1 us (84%)
  local copies, waits for them, and re-layouts  5.06 us (12%)
  between operations  1.29 us (3%)
    pallas_call x1, Pallas kernels, on_device(): pl.pallas_call(body, out_shape=(jax.ShapeDtypeStruct((n_cent, fb), f32),...  34.1 us
    unnamed x3, local copies, waits for them, and re-layouts  5.06 us

profile of v1, /device:TPU:0, one launch (start us, length us, event | category | flops | bytes accessed | tf_op | source)
XLA Modules:
  0.0 40.4 jit_solution(16739890741838262580)
XLA Ops:
  1.3 1.8 %copy.6.scales_ref = f32[1024,8]{1,0:T(8,128)} copy(f32[1024,8]{0,1:T(8,128)} %param.6) | data formatting | bytes 65536 | tf_op args[2]
  3.0 34.1 %shard_map.59 = (f32[1024,128]{1,0:T(8,128)}, f32[1,1024]{1,0:T(1,128)}) custom-call(bf16[2048,1024]{1,0:T(8,128)(2,1)} %rows_hbm.1, bf16[1024,1024]{1,0:T(8,128)(2,1)} %panel_hbm.1, f32[1024,8]{1,0:T(8,128)} %copy.6.scales_ref, s32[1]{0:T(128)S(6)} %copy.9.temp_ref), custom_call_target="tpu_custom_call" | custom-call | tf_op jit(solution)/shard_map/pallas_call | solution.py:254
  37.1 2.0 %copy.7 = f32[128,1024]{1,0:T(8,128)} copy(f32[128,1024]{0,1:T(8,128)} %bitcast.2) | data formatting | bytes 1048576
  39.2 1.3 %copy.10 = f32[1024]{0:T(1024)} copy(f32[1024]{0:T(1024)} %bitcast.3) | data formatting | bytes 8192

commit v2 on v1

--- a/solution.py
+++ b/solution.py
@@ -42,7 +42,7 @@
     n_rows, width = rows_ref.shape
     n_cent = cent_ref.shape[0]
     n = n_rows // n_chunks
-    n_blk = scales_ref.shape[1]
+    n_blk = scales_ref.shape[0]
     blk = width // n_blk
     fb = out_ref.shape[1]
     half = n_cent // 2
@@ -52,8 +52,12 @@
     z = lax.axis_index("cent")
     r = lax.axis_index("rep")
 
-    panel_copy = pltpu.make_async_copy(panel_hbm, panel_ref, panel_sem)
-    panel_copy.start()
+    panel_copies = []
+    for i, k in enumerate(range(0, n_cent, tile)):
+        cp = pltpu.make_async_copy(
+            panel_hbm.at[pl.ds(k, tile)], panel_ref.at[pl.ds(k, tile)], panel_sem.at[i])
+        cp.start()
+        panel_copies.append(cp)
     row_copies = []
     for c in range(n_chunks):
         cp = pltpu.make_async_copy(
@@ -72,12 +76,13 @@
 
     scale2 = temp_ref[0].astype(jnp.float32) * (math.log2(math.e) / math.sqrt(width))
 
-    panel_copy.wait()
-    for k in range(0, n_cent, tile):
+    scales = scales_ref[...].T
+    for i, k in enumerate(range(0, n_cent, tile)):
+        panel_copies[i].wait()
         sq = jnp.zeros((tile, blk), jnp.float32)
         for b in range(n_blk):
             full = panel_ref[k:k + tile, b * blk:(b + 1) * blk].astype(jnp.float32)
-            full = (full * scales_ref[k:k + tile, b:b + 1]).astype(jnp.bfloat16)
+            full = (full * scales[k:k + tile, b:b + 1]).astype(jnp.bfloat16)
             cent_ref[k:k + tile, b * blk:(b + 1) * blk] = full
             wide = full.astype(jnp.float32)
             sq = sq + wide * wide
@@ -88,13 +93,17 @@
 
     stat_copies = []
 
-    def logits_tile(c, k):
-        prod = lax.dot_general(cent_ref[k:k + tile, :], rows_ref[c * n:(c + 1) * n, :], NT,
+    def logits(c):
+        prod = lax.dot_general(cent_ref[...], rows_ref[c * n:(c + 1) * n, :], NT,
                                preferred_element_type=jnp.float32)
-        bias = jnp.concatenate([bias_ref[k:k + tile, :]] * (n // LANES), axis=1)
-        t = prod * scale2 + bias
-        t_refs[c][k:k + tile, :] = t
-        return jnp.max(t.reshape(tile // 8, 8, n), axis=0)
+        best = None
+        for k in range(0, n_cent, tile):
+            bias = jnp.concatenate([bias_ref[k:k + tile, :]] * (n // LANES), axis=1)
+            t = prod[k:k + tile, :] * scale2 + bias
+            t_refs[c][k:k + tile, :] = t
+            m = jnp.max(t.reshape(tile // 8, 8, n), axis=0)
+            best = m if best is None else jnp.maximum(best, m)
+        return jnp.max(best, axis=0, keepdims=True)
 
     def exp_tile(c, k, top):
         e = jnp.exp2(t_refs[c][k:k + tile, :] - top)
@@ -111,24 +120,7 @@
             cp.start()
             stat_copies.append(cp)
 
-    tops = [None] * n_chunks
-    for c in range(n_chunks + 1):
-        if c < n_chunks:
-            row_copies[c].wait()
-        best = total = None
-        for k in range(0, n_cent, tile):
-            if c < n_chunks:
-                m = logits_tile(c, k)
-                best = m if best is None else jnp.maximum(best, m)
-            if c > 0:
-                s = exp_tile(c - 1, k, tops[c - 1])
-                total = s if total is None else total + s
-        if c < n_chunks:
-            tops[c] = jnp.max(best, axis=0, keepdims=True)
-        if c > 0:
-            send_stats(c - 1, tops[c - 1], jnp.sum(total, axis=0, keepdims=True))
-
-    def weights(c):
+    def ratios(c):
         for cp in stat_copies[c * len(z_peers):(c + 1) * len(z_peers)]:
             cp.wait_recv()
         mine = stat_out[c, 0:1, :]
@@ -138,7 +130,9 @@
         total = stat_out[c, 1:2, :] * jnp.exp2(mine - top)
         for o in range(len(z_peers)):
             total = total + stat_in[c, o, 1:2, :] * jnp.exp2(stat_in[c, o, 0:1, :] - top)
-        ratio = jnp.exp2(mine - top) / total
+        return jnp.exp2(mine - top) / total
+
+    def weights(c, ratio):
         for k in range(0, n_cent, tile):
             w = t_refs[c][k:k + tile, :] * ratio
             w_ref[k:k + tile, c * n:(c + 1) * n] = w.astype(jnp.bfloat16)
@@ -149,6 +143,25 @@
                 part = part + cnt_ref[k:k + tile, :]
             cnt_ref[k:k + tile, :] = part
 
+    lag = 3
+    tops = []
+    for c in range(n_chunks + 1):
+        if c < n_chunks:
+            row_copies[c].wait()
+        if c >= lag:
+            ratio = ratios(c - lag)
+        if c < n_chunks:
+            tops.append(logits(c))
+        if c > 0:
+            total = None
+            for k in range(0, n_cent, tile):
+                part = exp_tile(c - 1, k, tops[c - 1])
+                total = part if total is None else total + part
+        if c >= lag:
+            weights(c - lag, ratio)
+        if c > 0:
+            send_stats(c - 1, tops[c - 1], jnp.sum(total, axis=0, keepdims=True))
+
     def columns(q):
         return pl.ds(pl.multiple_of(flip(d, q, bits) * (2 * fb), 2 * fb), 2 * fb)
 
@@ -167,9 +180,13 @@
 
     orders = [list(range(bits)), list(range(bits))[::-1]]
 
-    def unit(h, q):
-        split(h, q, lax.dot_general(w_ref[h * half:(h + 1) * half, :], rows_ref[:, columns(q)], NN,
-                                    preferred_element_type=jnp.float32))
+    def dot(start, stop, q):
+        return lax.dot_general(w_ref[:, start:stop], rows_ref[start:stop, columns(q)], NN,
+                               preferred_element_type=jnp.float32)
+
+    def unit(q, prod):
+        for h in range(2):
+            split(h, q, prod[h * half:(h + 1) * half])
 
     def finish(h, q):
         order = orders[h]
@@ -190,21 +207,14 @@
         cp.start()
         dp_copies[h, q] = cp
 
-    ranked = []
-    for order in orders:
-        ranked.append(sorted(range(dp_n), reverse=True,
-                             key=lambda q: [(q >> b) & 1 for b in order]))
-    todo = [(h, ranked[h][i]) for i in range(dp_n) for h in range(2)]
-
-    acc = None
-    h0, q0 = todo[0]
-    for c in range(n_chunks):
-        weights(c)
-        p = lax.dot_general(w_ref[h0 * half:(h0 + 1) * half, c * n:(c + 1) * n],
-                            rows_ref[c * n:(c + 1) * n, columns(q0)], NN,
-                            preferred_element_type=jnp.float32)
-        acc = p if acc is None else acc + p
-    split(h0, q0, acc)
+    ranked = [sorted(range(dp_n), reverse=True, key=lambda q: [(q >> b) & 1 for b in order])
+              for order in orders]
+
+    early = n_chunks + 1 - lag
+    prod = dot(0, early * n, ranked[0][0])
+    for c in range(early, n_chunks):
+        weights(c, ratios(c))
+    unit(ranked[0][0], prod + dot(early * n, n_rows, ranked[0][0]))
 
     cnt_out[...] = jnp.sum(cnt_ref[...].T, axis=0, keepdims=True)
     cnt_copies = []
@@ -215,14 +225,15 @@
         cp.start()
         cnt_copies.append(cp)
 
-    done = 0
-    for i in range(1, len(todo)):
-        unit(*todo[i])
-        h, q = todo[done]
-        if done < i and first_step(q, orders[h]) == 0:
-            finish(h, q)
-            done += 1
-    for h, q in todo[done:-2]:
+    for i in range(1, dp_n):
+        unit(ranked[0][i], dot(0, n_rows, ranked[0][i]))
+        for h in range(2):
+            if first_step(ranked[0][i - 1], orders[h]) == 0:
+                finish(h, ranked[0][i - 1])
+    later = [(first_step(q, orders[h]), i, h, q) for h in range(2)
+             for i, q in enumerate(ranked[h]) if first_step(q, orders[h]) > 0]
+    later.sort()
+    for _, _, h, q in later[:-2]:
         finish(h, q)
 
     counts = cnt_out[...]
@@ -231,18 +242,23 @@
         counts = counts + cnt_in[o]
     counts_ref[...] = counts
 
-    for h, q in todo[-2:]:
+    for _, _, h, q in later[-2:]:
         finish(h, q)
 
     for cp in stat_copies + cnt_copies + list(core_copies.values()) + list(dp_copies.values()):
         cp.wait_send()
+
+
+def place(sums_ref, counts_in, out_ref, counts_ref):
+    out_ref[...] = sums_ref[...].T
+    counts_ref[...] = counts_in[...]
 
 
 def on_device(sizes, rows, panel, scales, inv_temp):
     dp_n, cent_n, rep_n = sizes
     n_rows, width = rows.shape
     n_cent = panel.shape[0]
-    n_chunks = 4
+    n_chunks = 8
     tile = 256
     n = n_rows // n_chunks
     fb = width // (dp_n * rep_n)
@@ -274,7 +290,7 @@
             pltpu.VMEM((n_chunks, cent_n - 1, 2, n), f32),
             pltpu.VMEM((1, n_cent), f32),
             pltpu.VMEM((group, 1, n_cent), f32),
-            dma((n_chunks,)), dma,
+            dma((n_chunks,)), dma((n_cent // tile,)),
             dma((2, dp_n)), dma((2, dp_n)),
             dma((2, dp_n - 1)), dma((2, dp_n - 1)),
             dma((n_chunks, cent_n - 1)), dma((n_chunks, cent_n - 1)),
@@ -282,8 +298,14 @@
         ],
         compiler_params=pltpu.CompilerParams(
             collective_id=0, has_side_effects=True, vmem_limit_bytes=56 * 1024 * 1024),
-    )(rows, panel, scales, inv_temp)
-    return sums.T, counts.reshape(n_cent)
+    )(rows, panel, scales.T, inv_temp)
+    sums, counts = pl.pallas_call(
+        place,
+        out_shape=(jax.ShapeDtypeStruct((fb, n_cent), f32), jax.ShapeDtypeStruct((1, n_cent), f32)),
+        in_specs=[pl.BlockSpec(memory_space=pltpu.VMEM)] * 2,
+        out_specs=(pl.BlockSpec(memory_space=pltpu.VMEM),) * 2,
+    )(sums, counts)
+    return sums, counts.reshape(n_cent)
 
 
 def solution(mesh):

time: 40.8 us -> 48.5 us (1.19)
  Pallas kernels: 34.1 us -> 47 us
  local copies, waits for them, and re-layouts: 5.06 us -> 0 us
    pallas_call x1, Pallas kernels: 34.1 us -> 44.9 us  [on_device(): pl.pallas_call(body, out_shape=(jax.ShapeDtypeStruct((n_cent, fb), f32),...]
    unnamed x3 -> x0, local copies, waits for them, and re-layouts: 5.06 us -> none
    pallas_call x0 -> x1, Pallas kernels: none -> 2.04 us  [on_device(): pl.pallas_call(place, out_shape=(jax.ShapeDtypeStruct((fb, n_cent), f32),...]
where the time goes in v2:
time: 48.5 us; the launch traced here: 48.2 us
  Pallas kernels  47 us (97%)
  between operations  1.28 us (3%)
    pallas_call x1, Pallas kernels, on_device(): pl.pallas_call(body, out_shape=(jax.ShapeDtypeStruct((n_cent, fb), f32),...  44.9 us
    pallas_call x1, Pallas kernels, on_device(): pl.pallas_call(place, out_shape=(jax.ShapeDtypeStruct((fb, n_cent), f32),...  2.04 us

profile of v2, /device:TPU:0, one launch (start us, length us, event | category | flops | bytes accessed | tf_op | source)
XLA Modules:
  0.0 48.2 jit_solution(8368181916229978473)
XLA Ops:
  1.3 44.9 %shard_map.59 = (f32[1024,128]{1,0:T(8,128)}, f32[1,1024]{1,0:T(1,128)}) custom-call(bf16[2048,1024]{1,0:T(8,128)(2,1)} %rows_hbm.1, bf16[1024,1024]{1,0:T(8,128)(2,1)} %panel_hbm.1, f32[8,1024]{1,0:T(8,128)} %bitcast.2, s32[1]{0:T(128)S(6)} %copy.6.temp_ref), custom_call_target="tpu_custom_call" | custom-call | tf_op jit(solution)/shard_map/pallas_call | solution.py:270
  46.2 2.0 %shard_map.60 = (f32[128,1024]{1,0:T(8,128)}, f32[1,1024]{1,0:T(1,128)}) custom-call(f32[1024,128]{1,0:T(8,128)} %get-tuple-element.6.sums_ref, f32[1,1024]{1,0:T(1,128)} %get-tuple-element.7.counts_in), custom_call_target="tpu_custom_call" | custom-call | tf_op jit(solution)/shard_map/pallas_call | solution.py:302

commit v3 on v2

--- a/solution.py
+++ b/solution.py
@@ -93,17 +93,13 @@
 
     stat_copies = []
 
-    def logits(c):
-        prod = lax.dot_general(cent_ref[...], rows_ref[c * n:(c + 1) * n, :], NT,
+    def logits_tile(c, k):
+        prod = lax.dot_general(cent_ref[k:k + tile, :], rows_ref[c * n:(c + 1) * n, :], NT,
                                preferred_element_type=jnp.float32)
-        best = None
-        for k in range(0, n_cent, tile):
-            bias = jnp.concatenate([bias_ref[k:k + tile, :]] * (n // LANES), axis=1)
-            t = prod[k:k + tile, :] * scale2 + bias
-            t_refs[c][k:k + tile, :] = t
-            m = jnp.max(t.reshape(tile // 8, 8, n), axis=0)
-            best = m if best is None else jnp.maximum(best, m)
-        return jnp.max(best, axis=0, keepdims=True)
+        bias = jnp.concatenate([bias_ref[k:k + tile, :]] * (n // LANES), axis=1)
+        t = prod * scale2 + bias
+        t_refs[c][k:k + tile, :] = t
+        return jnp.max(t.reshape(tile // 8, 8, n), axis=0)
 
     def exp_tile(c, k, top):
         e = jnp.exp2(t_refs[c][k:k + tile, :] - top)
@@ -132,16 +128,19 @@
             total = total + stat_in[c, o, 1:2, :] * jnp.exp2(stat_in[c, o, 0:1, :] - top)
         return jnp.exp2(mine - top) / total
 
+    def weights_tile(c, k, ratio):
+        w = t_refs[c][k:k + tile, :] * ratio
+        w_ref[k:k + tile, c * n:(c + 1) * n] = w.astype(jnp.bfloat16)
+        part = w[:, :LANES]
+        for l in range(LANES, n, LANES):
+            part = part + w[:, l:l + LANES]
+        if c > 0:
+            part = part + cnt_ref[k:k + tile, :]
+        cnt_ref[k:k + tile, :] = part
+
     def weights(c, ratio):
         for k in range(0, n_cent, tile):
-            w = t_refs[c][k:k + tile, :] * ratio
-            w_ref[k:k + tile, c * n:(c + 1) * n] = w.astype(jnp.bfloat16)
-            part = w[:, :LANES]
-            for l in range(LANES, n, LANES):
-                part = part + w[:, l:l + LANES]
-            if c > 0:
-                part = part + cnt_ref[k:k + tile, :]
-            cnt_ref[k:k + tile, :] = part
+            weights_tile(c, k, ratio)
 
     lag = 3
     tops = []
@@ -150,15 +149,18 @@
             row_copies[c].wait()
         if c >= lag:
             ratio = ratios(c - lag)
-        if c < n_chunks:
-            tops.append(logits(c))
-        if c > 0:
-            total = None
-            for k in range(0, n_cent, tile):
+        best = total = None
+        for k in range(0, n_cent, tile):
+            if c < n_chunks:
+                m = logits_tile(c, k)
+                best = m if best is None else jnp.maximum(best, m)
+            if c > 0:
                 part = exp_tile(c - 1, k, tops[c - 1])
                 total = part if total is None else total + part
-        if c >= lag:
-            weights(c - lag, ratio)
+            if c >= lag:
+                weights_tile(c - lag, k, ratio)
+        if c < n_chunks:
+            tops.append(jnp.max(best, axis=0, keepdims=True))
         if c > 0:
             send_stats(c - 1, tops[c - 1], jnp.sum(total, axis=0, keepdims=True))
 
@@ -168,25 +170,25 @@
     core_copies = {}
     dp_copies = {}
 
-    def split(h, q, prod):
-        first = r == 0
-        own_ref[h, q] = jnp.where(first, prod[:, :fb], prod[:, fb:])
-        core_out[h, q] = jnp.where(first, prod[:, fb:], prod[:, :fb]).astype(jnp.bfloat16)
-        cp = pltpu.make_async_remote_copy(
-            core_out.at[h, q], core_in.at[h, q], core_ss.at[h, q], core_rs.at[h, q],
-            device_id={"rep": 1 - r}, device_id_type=MESH)
-        cp.start()
-        core_copies[h, q] = cp
-
+    first = r == 0
     orders = [list(range(bits)), list(range(bits))[::-1]]
 
-    def dot(start, stop, q):
-        return lax.dot_general(w_ref[:, start:stop], rows_ref[start:stop, columns(q)], NN,
+    def dot(start, stop, k, q):
+        return lax.dot_general(w_ref[k:k + tile, start:stop], rows_ref[start:stop, columns(q)], NN,
                                preferred_element_type=jnp.float32)
 
-    def unit(q, prod):
+    def unit(q):
         for h in range(2):
-            split(h, q, prod[h * half:(h + 1) * half])
+            for k in range(0, half, tile):
+                prod = dot(0, n_rows, h * half + k, q)
+                own_ref[h, q, k:k + tile, :] = jnp.where(first, prod[:, :fb], prod[:, fb:])
+                core_out[h, q, k:k + tile, :] = jnp.where(
+                    first, prod[:, fb:], prod[:, :fb]).astype(jnp.bfloat16)
+            cp = pltpu.make_async_remote_copy(
+                core_out.at[h, q], core_in.at[h, q], core_ss.at[h, q], core_rs.at[h, q],
+                device_id={"rep": 1 - r}, device_id_type=MESH)
+            cp.start()
+            core_copies[h, q] = cp
 
     def finish(h, q):
         order = orders[h]
@@ -210,11 +212,9 @@
     ranked = [sorted(range(dp_n), reverse=True, key=lambda q: [(q >> b) & 1 for b in order])
               for order in orders]
 
-    early = n_chunks + 1 - lag
-    prod = dot(0, early * n, ranked[0][0])
-    for c in range(early, n_chunks):
+    for c in range(n_chunks + 1 - lag, n_chunks):
         weights(c, ratios(c))
-    unit(ranked[0][0], prod + dot(early * n, n_rows, ranked[0][0]))
+    unit(ranked[0][0])
 
     cnt_out[...] = jnp.sum(cnt_ref[...].T, axis=0, keepdims=True)
     cnt_copies = []
@@ -226,7 +226,7 @@
         cnt_copies.append(cp)
 
     for i in range(1, dp_n):
-        unit(ranked[0][i], dot(0, n_rows, ranked[0][i]))
+        unit(ranked[0][i])
         for h in range(2):
             if first_step(ranked[0][i - 1], orders[h]) == 0:
                 finish(h, ranked[0][i - 1])

time: 48.5 us -> 43.3 us (0.89)
  Pallas kernels: 47 us -> 41.8 us
    pallas_call x1, Pallas kernels: 44.9 us -> 39.8 us  [on_device(): pl.pallas_call(body, out_shape=(jax.ShapeDtypeStruct((n_cent, fb), f32),...]
where the time goes in v3:
time: 43.3 us; the launch traced here: 43.1 us
  Pallas kernels  41.8 us (97%)
  between operations  1.28 us (3%)
    pallas_call x1, Pallas kernels, on_device(): pl.pallas_call(body, out_shape=(jax.ShapeDtypeStruct((n_cent, fb), f32),...  39.8 us
    pallas_call x1, Pallas kernels, on_device(): pl.pallas_call(place, out_shape=(jax.ShapeDtypeStruct((fb, n_cent), f32),...  2.04 us

profile of v3, /device:TPU:0, one launch (start us, length us, event | category | flops | bytes accessed | tf_op | source)
XLA Modules:
  0.0 43.1 jit_solution(3428424435705116909)
XLA Ops:
  1.3 39.8 %shard_map.59 = (f32[1024,128]{1,0:T(8,128)}, f32[1,1024]{1,0:T(1,128)}) custom-call(bf16[2048,1024]{1,0:T(8,128)(2,1)} %rows_hbm.1, bf16[1024,1024]{1,0:T(8,128)(2,1)} %panel_hbm.1, f32[8,1024]{1,0:T(8,128)} %bitcast.2, s32[1]{0:T(128)S(6)} %copy.6.temp_ref), custom_call_target="tpu_custom_call" | custom-call | tf_op jit(solution)/shard_map/pallas_call | solution.py:270
  41.0 2.0 %shard_map.60 = (f32[128,1024]{1,0:T(8,128)}, f32[1,1024]{1,0:T(1,128)}) custom-call(f32[1024,128]{1,0:T(8,128)} %get-tuple-element.6.sums_ref, f32[1,1024]{1,0:T(1,128)} %get-tuple-element.7.counts_in), custom_call_target="tpu_custom_call" | custom-call | tf_op jit(solution)/shard_map/pallas_call | solution.py:302

commit v4 on v3

--- a/solution.py
+++ b/solution.py
@@ -35,7 +35,7 @@
     scratch = list(scratch)
     rows_ref, panel_ref, cent_ref, bias_ref, w_ref, cnt_ref = scratch[:6]
     t_refs = scratch[6:6 + n_chunks]
-    (own_ref, core_out, core_in, dp_out, dp_in, stat_out, stat_in, cnt_out, cnt_in,
+    (early_ref, own_ref, core_out, core_in, dp_out, dp_in, stat_out, stat_in, cnt_out, cnt_in,
      rows_sem, panel_sem, core_ss, core_rs, dp_ss, dp_rs, stat_ss, stat_rs,
      cnt_ss, cnt_rs) = scratch[6 + n_chunks:]
 
@@ -142,13 +142,10 @@
         for k in range(0, n_cent, tile):
             weights_tile(c, k, ratio)
 
-    lag = 3
     tops = []
     for c in range(n_chunks + 1):
         if c < n_chunks:
             row_copies[c].wait()
-        if c >= lag:
-            ratio = ratios(c - lag)
         best = total = None
         for k in range(0, n_cent, tile):
             if c < n_chunks:
@@ -157,8 +154,6 @@
             if c > 0:
                 part = exp_tile(c - 1, k, tops[c - 1])
                 total = part if total is None else total + part
-            if c >= lag:
-                weights_tile(c - lag, k, ratio)
         if c < n_chunks:
             tops.append(jnp.max(best, axis=0, keepdims=True))
         if c > 0:
@@ -173,22 +168,23 @@
     first = r == 0
     orders = [list(range(bits)), list(range(bits))[::-1]]
 
-    def dot(start, stop, k, q):
-        return lax.dot_general(w_ref[k:k + tile, start:stop], rows_ref[start:stop, columns(q)], NN,
+    def dot(start, stop, h, q):
+        return lax.dot_general(w_ref[h * half:(h + 1) * half, start:stop],
+                               rows_ref[start:stop, columns(q)], NN,
                                preferred_element_type=jnp.float32)
+
+    def split(h, q, prod):
+        own_ref[h, q] = jnp.where(first, prod[:, :fb], prod[:, fb:])
+        core_out[h, q] = jnp.where(first, prod[:, fb:], prod[:, :fb]).astype(jnp.bfloat16)
+        cp = pltpu.make_async_remote_copy(
+            core_out.at[h, q], core_in.at[h, q], core_ss.at[h, q], core_rs.at[h, q],
+            device_id={"rep": 1 - r}, device_id_type=MESH)
+        cp.start()
+        core_copies[h, q] = cp
 
     def unit(q):
         for h in range(2):
-            for k in range(0, half, tile):
-                prod = dot(0, n_rows, h * half + k, q)
-                own_ref[h, q, k:k + tile, :] = jnp.where(first, prod[:, :fb], prod[:, fb:])
-                core_out[h, q, k:k + tile, :] = jnp.where(
-                    first, prod[:, fb:], prod[:, :fb]).astype(jnp.bfloat16)
-            cp = pltpu.make_async_remote_copy(
-                core_out.at[h, q], core_in.at[h, q], core_ss.at[h, q], core_rs.at[h, q],
-                device_id={"rep": 1 - r}, device_id_type=MESH)
-            cp.start()
-            core_copies[h, q] = cp
+            split(h, q, dot(0, n_rows, h, q))
 
     def finish(h, q):
         order = orders[h]
@@ -212,9 +208,18 @@
     ranked = [sorted(range(dp_n), reverse=True, key=lambda q: [(q >> b) & 1 for b in order])
               for order in orders]
 
-    for c in range(n_chunks + 1 - lag, n_chunks):
+    q0 = ranked[0][0]
+    cut = (n_chunks - 1) * n
+    for c in range(n_chunks - 1):
         weights(c, ratios(c))
-    unit(ranked[0][0])
+    early = [dot(0, cut, h, q0) for h in range(2)]
+    for h in range(2):
+        own_ref[h, q0] = early[h][:, :fb]
+        early_ref[h] = early[h][:, fb:]
+    weights(n_chunks - 1, ratios(n_chunks - 1))
+    for h in range(2):
+        prod = jnp.concatenate([own_ref[h, q0], early_ref[h]], axis=1)
+        split(h, q0, prod + dot(cut, n_rows, h, q0))
 
     cnt_out[...] = jnp.sum(cnt_ref[...].T, axis=0, keepdims=True)
     cnt_copies = []
@@ -258,7 +263,7 @@
     dp_n, cent_n, rep_n = sizes
     n_rows, width = rows.shape
     n_cent = panel.shape[0]
-    n_chunks = 8
+    n_chunks = 4
     tile = 256
     n = n_rows // n_chunks
     fb = width // (dp_n * rep_n)
@@ -281,6 +286,7 @@
             pltpu.VMEM((n_cent, n_rows), bf16),
             pltpu.VMEM((n_cent, LANES), f32),
             *[pltpu.VMEM((n_cent, n), f32) for _ in range(n_chunks)],
+            pltpu.VMEM((2, half, fb), f32),
             pltpu.VMEM((2, dp_n, half, fb), f32),
             pltpu.VMEM((2, dp_n, half, fb), bf16),
             pltpu.VMEM((2, dp_n, half, fb), bf16),

time: 43.3 us -> 37.5 us (0.87)
  Pallas kernels: 41.8 us -> 36 us
    pallas_call x1, Pallas kernels: 39.8 us -> 33.9 us  [on_device(): pl.pallas_call(body, out_shape=(jax.ShapeDtypeStruct((n_cent, fb), f32),...]
where the time goes in v4:
time: 37.5 us; the launch traced here: 37.3 us
  Pallas kernels  36 us (96%)
  between operations  1.28 us (3%)
    pallas_call x1, Pallas kernels, on_device(): pl.pallas_call(body, out_shape=(jax.ShapeDtypeStruct((n_cent, fb), f32),...  33.9 us
    pallas_call x1, Pallas kernels, on_device(): pl.pallas_call(place, out_shape=(jax.ShapeDtypeStruct((fb, n_cent), f32),...  2.04 us

profile of v4, /device:TPU:0, one launch (start us, length us, event | category | flops | bytes accessed | tf_op | source)
XLA Modules:
  0.0 37.3 jit_solution(7630490736114465349)
XLA Ops:
  1.3 33.9 %shard_map.59 = (f32[1024,128]{1,0:T(8,128)}, f32[1,1024]{1,0:T(1,128)}) custom-call(bf16[2048,1024]{1,0:T(8,128)(2,1)} %rows_hbm.1, bf16[1024,1024]{1,0:T(8,128)(2,1)} %panel_hbm.1, f32[8,1024]{1,0:T(8,128)} %bitcast.2, s32[1]{0:T(128)S(6)} %copy.6.temp_ref), custom_call_target="tpu_custom_call" | custom-call | tf_op jit(solution)/shard_map/pallas_call | solution.py:275
  35.2 2.0 %shard_map.60 = (f32[128,1024]{1,0:T(8,128)}, f32[1,1024]{1,0:T(1,128)}) custom-call(f32[1024,128]{1,0:T(8,128)} %get-tuple-element.6.sums_ref, f32[1,1024]{1,0:T(1,128)} %get-tuple-element.7.counts_in), custom_call_target="tpu_custom_call" | custom-call | tf_op jit(solution)/shard_map/pallas_call | solution.py:308

commit v5 on v4

--- a/solution.py
+++ b/solution.py
@@ -52,14 +52,18 @@
     z = lax.axis_index("cent")
     r = lax.axis_index("rep")
 
+    first_rows = pltpu.make_async_copy(
+        rows_hbm.at[pl.ds(0, n)], rows_ref.at[pl.ds(0, n)], rows_sem.at[0])
     panel_copies = []
     for i, k in enumerate(range(0, n_cent, tile)):
         cp = pltpu.make_async_copy(
             panel_hbm.at[pl.ds(k, tile)], panel_ref.at[pl.ds(k, tile)], panel_sem.at[i])
         cp.start()
         panel_copies.append(cp)
-    row_copies = []
-    for c in range(n_chunks):
+        if i == 0:
+            first_rows.start()
+    row_copies = [first_rows]
+    for c in range(1, n_chunks):
         cp = pltpu.make_async_copy(
             rows_hbm.at[pl.ds(c * n, n)], rows_ref.at[pl.ds(c * n, n)], rows_sem.at[c])
         cp.start()
@@ -77,8 +81,9 @@
     scale2 = temp_ref[0].astype(jnp.float32) * (math.log2(math.e) / math.sqrt(width))
 
     scales = scales_ref[...].T
-    for i, k in enumerate(range(0, n_cent, tile)):
-        panel_copies[i].wait()
+
+    def centroids_tile(k):
+        panel_copies[k // tile].wait()
         sq = jnp.zeros((tile, blk), jnp.float32)
         for b in range(n_blk):
             full = panel_ref[k:k + tile, b * blk:(b + 1) * blk].astype(jnp.float32)
@@ -88,8 +93,6 @@
             sq = sq + wide * wide
         norm = jnp.sum(sq, axis=1, keepdims=True)
         bias_ref[k:k + tile, :] = jnp.broadcast_to((-0.5 * scale2) * norm, (tile, LANES))
-
-    pl.semaphore_wait(barrier, len(z_peers) + len(group))
 
     stat_copies = []
 
@@ -143,19 +146,28 @@
             weights_tile(c, k, ratio)
 
     tops = []
+    centroids_tile(0)
     for c in range(n_chunks + 1):
         if c < n_chunks:
             row_copies[c].wait()
+        if c >= 3:
+            ratio = ratios(c - 3)
         best = total = None
         for k in range(0, n_cent, tile):
+            if c == 0 and k + tile < n_cent:
+                centroids_tile(k + tile)
             if c < n_chunks:
                 m = logits_tile(c, k)
                 best = m if best is None else jnp.maximum(best, m)
             if c > 0:
                 part = exp_tile(c - 1, k, tops[c - 1])
                 total = part if total is None else total + part
+            if c >= 3:
+                weights_tile(c - 3, k, ratio)
         if c < n_chunks:
             tops.append(jnp.max(best, axis=0, keepdims=True))
+        if c == 1:
+            pl.semaphore_wait(barrier, len(z_peers) + len(group))
         if c > 0:
             send_stats(c - 1, tops[c - 1], jnp.sum(total, axis=0, keepdims=True))
 
@@ -181,10 +193,6 @@
             device_id={"rep": 1 - r}, device_id_type=MESH)
         cp.start()
         core_copies[h, q] = cp
-
-    def unit(q):
-        for h in range(2):
-            split(h, q, dot(0, n_rows, h, q))
 
     def finish(h, q):
         order = orders[h]
@@ -209,17 +217,20 @@
               for order in orders]
 
     q0 = ranked[0][0]
-    cut = (n_chunks - 1) * n
-    for c in range(n_chunks - 1):
-        weights(c, ratios(c))
-    early = [dot(0, cut, h, q0) for h in range(2)]
-    for h in range(2):
-        own_ref[h, q0] = early[h][:, :fb]
-        early_ref[h] = early[h][:, fb:]
-    weights(n_chunks - 1, ratios(n_chunks - 1))
-    for h in range(2):
-        prod = jnp.concatenate([own_ref[h, q0], early_ref[h]], axis=1)
-        split(h, q0, prod + dot(cut, n_rows, h, q0))
+    known = n_chunks - 2
+    steps = [(0, known * n)] + [(c * n, (c + 1) * n) for c in range(known, n_chunks)]
+    for i, (start, stop) in enumerate(steps):
+        if i > 0:
+            c = known + i - 1
+            weights(c, ratios(c))
+        for h in range(2):
+            prod = dot(start, stop, h, q0)
+            if i > 0:
+                prod = prod + early_ref[h]
+            if i < len(steps) - 1:
+                early_ref[h] = prod
+            else:
+                split(h, q0, prod)
 
     cnt_out[...] = jnp.sum(cnt_ref[...].T, axis=0, keepdims=True)
     cnt_copies = []
@@ -231,8 +242,8 @@
         cnt_copies.append(cp)
 
     for i in range(1, dp_n):
-        unit(ranked[0][i])
         for h in range(2):
+            split(h, ranked[0][i], dot(0, n_rows, h, ranked[0][i]))
             if first_step(ranked[0][i - 1], orders[h]) == 0:
                 finish(h, ranked[0][i - 1])
     later = [(first_step(q, orders[h]), i, h, q) for h in range(2)
@@ -286,7 +297,7 @@
             pltpu.VMEM((n_cent, n_rows), bf16),
             pltpu.VMEM((n_cent, LANES), f32),
             *[pltpu.VMEM((n_cent, n), f32) for _ in range(n_chunks)],
-            pltpu.VMEM((2, half, fb), f32),
+            pltpu.VMEM((2, half, 2 * fb), f32),
             pltpu.VMEM((2, dp_n, half, fb), f32),
             pltpu.VMEM((2, dp_n, half, fb), bf16),
             pltpu.VMEM((2, dp_n, half, fb), bf16),

time: 37.5 us -> 37.4 us (level)
  no operation moved by 1% of the time
where the time goes in v5:
time: 37.4 us; the launch traced here: 37.2 us
  Pallas kernels  35.9 us (96%)
  between operations  1.28 us (3%)
    pallas_call x1, Pallas kernels, on_device(): pl.pallas_call(body, out_shape=(jax.ShapeDtypeStruct((n_cent, fb), f32),...  33.9 us
    pallas_call x1, Pallas kernels, on_device(): pl.pallas_call(place, out_shape=(jax.ShapeDtypeStruct((fb, n_cent), f32),...  2.04 us

profile of v5, /device:TPU:0, one launch (start us, length us, event | category | flops | bytes accessed | tf_op | source)
XLA Modules:
  0.0 37.2 jit_solution(5443848481063680862)
XLA Ops:
  1.3 33.9 %shard_map.59 = (f32[1024,128]{1,0:T(8,128)}, f32[1,1024]{1,0:T(1,128)}) custom-call(bf16[2048,1024]{1,0:T(8,128)(2,1)} %rows_hbm.1, bf16[1024,1024]{1,0:T(8,128)(2,1)} %panel_hbm.1, f32[8,1024]{1,0:T(8,128)} %bitcast.2, s32[1]{0:T(128)S(6)} %copy.6.temp_ref), custom_call_target="tpu_custom_call" | custom-call | tf_op jit(solution)/shard_map/pallas_call | solution.py:286
  35.2 2.0 %shard_map.60 = (f32[128,1024]{1,0:T(8,128)}, f32[1,1024]{1,0:T(1,128)}) custom-call(f32[1024,128]{1,0:T(8,128)} %get-tuple-element.6.sums_ref, f32[1,1024]{1,0:T(1,128)} %get-tuple-element.7.counts_in), custom_call_target="tpu_custom_call" | custom-call | tf_op jit(solution)/shard_map/pallas_call | solution.py:319

commit v6 on v5

--- a/solution.py
+++ b/solution.py
@@ -33,11 +33,11 @@
            out_ref, counts_ref, *scratch):
     n_chunks, tile = parts
     scratch = list(scratch)
-    rows_ref, panel_ref, cent_ref, bias_ref, w_ref, cnt_ref = scratch[:6]
-    t_refs = scratch[6:6 + n_chunks]
+    rows_ref, panel_ref, cent_ref, bias_ref, w_ref, cnt_ref, scales_t = scratch[:7]
+    t_refs = scratch[7:7 + n_chunks]
     (early_ref, own_ref, core_out, core_in, dp_out, dp_in, stat_out, stat_in, cnt_out, cnt_in,
      rows_sem, panel_sem, core_ss, core_rs, dp_ss, dp_rs, stat_ss, stat_rs,
-     cnt_ss, cnt_rs) = scratch[6 + n_chunks:]
+     cnt_ss, cnt_rs) = scratch[7 + n_chunks:]
 
     n_rows, width = rows_ref.shape
     n_cent = cent_ref.shape[0]
@@ -82,31 +82,43 @@
 
     scales = scales_ref[...].T
 
-    def centroids_tile(k):
-        panel_copies[k // tile].wait()
+    scales_t[:, :n_blk] = scales
+    for cp in panel_copies:
+        cp.wait()
+
+    def at(i):
+        return pl.ds(pl.multiple_of(i * tile, tile), tile)
+
+    def each_tile(body, init=0):
+        return lax.fori_loop(0, n_cent // tile, body, init)
+
+    def centroids_tile(i, carry):
         sq = jnp.zeros((tile, blk), jnp.float32)
         for b in range(n_blk):
-            full = panel_ref[k:k + tile, b * blk:(b + 1) * blk].astype(jnp.float32)
-            full = (full * scales[k:k + tile, b:b + 1]).astype(jnp.bfloat16)
-            cent_ref[k:k + tile, b * blk:(b + 1) * blk] = full
+            full = panel_ref[at(i), b * blk:(b + 1) * blk].astype(jnp.float32)
+            full = (full * scales_t[at(i), b:b + 1]).astype(jnp.bfloat16)
+            cent_ref[at(i), b * blk:(b + 1) * blk] = full
             wide = full.astype(jnp.float32)
             sq = sq + wide * wide
         norm = jnp.sum(sq, axis=1, keepdims=True)
-        bias_ref[k:k + tile, :] = jnp.broadcast_to((-0.5 * scale2) * norm, (tile, LANES))
+        bias_ref[at(i), :] = jnp.broadcast_to((-0.5 * scale2) * norm, (tile, LANES))
+        return carry
+
+    each_tile(centroids_tile)
 
     stat_copies = []
 
-    def logits_tile(c, k):
-        prod = lax.dot_general(cent_ref[k:k + tile, :], rows_ref[c * n:(c + 1) * n, :], NT,
+    def logits_tile(c, i):
+        prod = lax.dot_general(cent_ref[at(i), :], rows_ref[c * n:(c + 1) * n, :], NT,
                                preferred_element_type=jnp.float32)
-        bias = jnp.concatenate([bias_ref[k:k + tile, :]] * (n // LANES), axis=1)
+        bias = jnp.concatenate([bias_ref[at(i), :]] * (n // LANES), axis=1)
         t = prod * scale2 + bias
-        t_refs[c][k:k + tile, :] = t
+        t_refs[c][at(i), :] = t
         return jnp.max(t.reshape(tile // 8, 8, n), axis=0)
 
-    def exp_tile(c, k, top):
-        e = jnp.exp2(t_refs[c][k:k + tile, :] - top)
-        t_refs[c][k:k + tile, :] = e
+    def exp_tile(c, i, top):
+        e = jnp.exp2(t_refs[c][at(i), :] - top)
+        t_refs[c][at(i), :] = e
         return jnp.sum(e.reshape(tile // 8, 8, n), axis=0)
 
     def send_stats(c, top, total):
@@ -131,39 +143,40 @@
             total = total + stat_in[c, o, 1:2, :] * jnp.exp2(stat_in[c, o, 0:1, :] - top)
         return jnp.exp2(mine - top) / total
 
-    def weights_tile(c, k, ratio):
-        w = t_refs[c][k:k + tile, :] * ratio
-        w_ref[k:k + tile, c * n:(c + 1) * n] = w.astype(jnp.bfloat16)
+    def weights_tile(c, i, ratio):
+        w = t_refs[c][at(i), :] * ratio
+        w_ref[at(i), c * n:(c + 1) * n] = w.astype(jnp.bfloat16)
         part = w[:, :LANES]
         for l in range(LANES, n, LANES):
             part = part + w[:, l:l + LANES]
         if c > 0:
-            part = part + cnt_ref[k:k + tile, :]
-        cnt_ref[k:k + tile, :] = part
+            part = part + cnt_ref[at(i), :]
+        cnt_ref[at(i), :] = part
 
     def weights(c, ratio):
-        for k in range(0, n_cent, tile):
-            weights_tile(c, k, ratio)
+        def body(i, carry):
+            weights_tile(c, i, ratio)
+            return carry
+        each_tile(body)
 
     tops = []
-    centroids_tile(0)
     for c in range(n_chunks + 1):
         if c < n_chunks:
             row_copies[c].wait()
-        if c >= 3:
-            ratio = ratios(c - 3)
-        best = total = None
-        for k in range(0, n_cent, tile):
-            if c == 0 and k + tile < n_cent:
-                centroids_tile(k + tile)
+        ratio = ratios(c - 3) if c >= 3 else None
+
+        def body(i, carry, c=c, ratio=ratio):
+            best, total = carry
             if c < n_chunks:
-                m = logits_tile(c, k)
-                best = m if best is None else jnp.maximum(best, m)
+                best = jnp.maximum(best, logits_tile(c, i))
             if c > 0:
-                part = exp_tile(c - 1, k, tops[c - 1])
-                total = part if total is None else total + part
+                total = total + exp_tile(c - 1, i, tops[c - 1])
             if c >= 3:
-                weights_tile(c - 3, k, ratio)
+                weights_tile(c - 3, i, ratio)
+            return best, total
+
+        best, total = each_tile(
+            body, (jnp.full((8, n), -jnp.inf, jnp.float32), jnp.zeros((8, n), jnp.float32)))
         if c < n_chunks:
             tops.append(jnp.max(best, axis=0, keepdims=True))
         if c == 1:
@@ -180,19 +193,29 @@
     first = r == 0
     orders = [list(range(bits)), list(range(bits))[::-1]]
 
-    def dot(start, stop, h, q):
-        return lax.dot_general(w_ref[h * half:(h + 1) * half, start:stop],
-                               rows_ref[start:stop, columns(q)], NN,
-                               preferred_element_type=jnp.float32)
-
-    def split(h, q, prod):
-        own_ref[h, q] = jnp.where(first, prod[:, :fb], prod[:, fb:])
-        core_out[h, q] = jnp.where(first, prod[:, fb:], prod[:, :fb]).astype(jnp.bfloat16)
-        cp = pltpu.make_async_remote_copy(
-            core_out.at[h, q], core_in.at[h, q], core_ss.at[h, q], core_rs.at[h, q],
-            device_id={"rep": 1 - r}, device_id_type=MESH)
-        cp.start()
-        core_copies[h, q] = cp
+    def dot(start, stop, h, q, last, add):
+        def body(i, carry):
+            at_i = pl.ds(pl.multiple_of(i * tile, tile), tile)
+            at_w = pl.ds(pl.multiple_of(h * half + i * tile, tile), tile)
+            prod = lax.dot_general(w_ref[at_w, start:stop], rows_ref[start:stop, columns(q)], NN,
+                                   preferred_element_type=jnp.float32)
+            if add:
+                prod = prod + early_ref[h, at_i, :]
+            if not last:
+                early_ref[h, at_i, :] = prod
+            else:
+                own_ref[h, q, at_i, :] = jnp.where(first, prod[:, :fb], prod[:, fb:])
+                core_out[h, q, at_i, :] = jnp.where(
+                    first, prod[:, fb:], prod[:, :fb]).astype(jnp.bfloat16)
+            return carry
+
+        lax.fori_loop(0, half // tile, body, 0)
+        if last:
+            cp = pltpu.make_async_remote_copy(
+                core_out.at[h, q], core_in.at[h, q], core_ss.at[h, q], core_rs.at[h, q],
+                device_id={"rep": 1 - r}, device_id_type=MESH)
+            cp.start()
+            core_copies[h, q] = cp
 
     def finish(h, q):
         order = orders[h]
@@ -224,13 +247,7 @@
             c = known + i - 1
             weights(c, ratios(c))
         for h in range(2):
-            prod = dot(start, stop, h, q0)
-            if i > 0:
-                prod = prod + early_ref[h]
-            if i < len(steps) - 1:
-                early_ref[h] = prod
-            else:
-                split(h, q0, prod)
+            dot(start, stop, h, q0, i == len(steps) - 1, i > 0)
 
     cnt_out[...] = jnp.sum(cnt_ref[...].T, axis=0, keepdims=True)
     cnt_copies = []
@@ -243,7 +260,7 @@
 
     for i in range(1, dp_n):
         for h in range(2):
-            split(h, ranked[0][i], dot(0, n_rows, h, ranked[0][i]))
+            dot(0, n_rows, h, ranked[0][i], True, False)
             if first_step(ranked[0][i - 1], orders[h]) == 0:
                 finish(h, ranked[0][i - 1])
     later = [(first_step(q, orders[h]), i, h, q) for h in range(2)
@@ -295,6 +312,7 @@
             pltpu.VMEM((n_cent, width), bf16),
             pltpu.VMEM((n_cent, LANES), f32),
             pltpu.VMEM((n_cent, n_rows), bf16),
+            pltpu.VMEM((n_cent, LANES), f32),
             pltpu.VMEM((n_cent, LANES), f32),
             *[pltpu.VMEM((n_cent, n), f32) for _ in range(n_chunks)],
             pltpu.VMEM((2, half, 2 * fb), f32),

time: 37.4 us -> 41.2 us (1.10)
  Pallas kernels: 35.9 us -> 39.7 us
    pallas_call x1, Pallas kernels: 33.9 us -> 37.7 us  [on_device(): pl.pallas_call(body, out_shape=(jax.ShapeDtypeStruct((n_cent, fb), f32),...]
where the time goes in v6:
time: 41.2 us; the launch traced here: 41 us
  Pallas kernels  39.7 us (96%)
  between operations  1.28 us (3%)
    pallas_call x1, Pallas kernels, on_device(): pl.pallas_call(body, out_shape=(jax.ShapeDtypeStruct((n_cent, fb), f32),...  37.7 us
    pallas_call x1, Pallas kernels, on_device(): pl.pallas_call(place, out_shape=(jax.ShapeDtypeStruct((fb, n_cent), f32),...  2.04 us

profile of v6, /device:TPU:0, one launch (start us, length us, event | category | flops | bytes accessed | tf_op | source)
XLA Modules:
  0.0 41.0 jit_solution(12817881369419102378)
XLA Ops:
  1.3 37.7 %shard_map.59 = (f32[1024,128]{1,0:T(8,128)}, f32[1,1024]{1,0:T(1,128)}) custom-call(bf16[2048,1024]{1,0:T(8,128)(2,1)} %rows_hbm.1, bf16[1024,1024]{1,0:T(8,128)(2,1)} %panel_hbm.1, f32[8,1024]{1,0:T(8,128)} %bitcast.2, s32[1]{0:T(128)S(6)} %copy.6.temp_ref), custom_call_target="tpu_custom_call" | custom-call | tf_op jit(solution)/shard_map/pallas_call | solution.py:303
  38.9 2.0 %shard_map.60 = (f32[128,1024]{1,0:T(8,128)}, f32[1,1024]{1,0:T(1,128)}) custom-call(f32[1024,128]{1,0:T(8,128)} %get-tuple-element.6.sums_ref, f32[1,1024]{1,0:T(1,128)} %get-tuple-element.7.counts_in), custom_call_target="tpu_custom_call" | custom-call | tf_op jit(solution)/shard_map/pallas_call | solution.py:337

commit v7 on v5

--- a/solution.py
+++ b/solution.py
@@ -96,13 +96,16 @@
 
     stat_copies = []
 
-    def logits_tile(c, k):
-        prod = lax.dot_general(cent_ref[k:k + tile, :], rows_ref[c * n:(c + 1) * n, :], NT,
+    tall, wide_n = 2 * tile, n // 2
+
+    def logits_tile(c, k, col):
+        prod = lax.dot_general(cent_ref[k:k + tall, :],
+                               rows_ref[c * n + col:c * n + col + wide_n, :], NT,
                                preferred_element_type=jnp.float32)
-        bias = jnp.concatenate([bias_ref[k:k + tile, :]] * (n // LANES), axis=1)
+        bias = jnp.concatenate([bias_ref[k:k + tall, :]] * (wide_n // LANES), axis=1)
         t = prod * scale2 + bias
-        t_refs[c][k:k + tile, :] = t
-        return jnp.max(t.reshape(tile // 8, 8, n), axis=0)
+        t_refs[c][k:k + tall, col:col + wide_n] = t
+        return jnp.max(t.reshape(tall // 8, 8, wide_n), axis=0)
 
     def exp_tile(c, k, top):
         e = jnp.exp2(t_refs[c][k:k + tile, :] - top)
@@ -146,26 +149,29 @@
             weights_tile(c, k, ratio)
 
     tops = []
-    centroids_tile(0)
+    for k in range(0, tall, tile):
+        centroids_tile(k)
     for c in range(n_chunks + 1):
         if c < n_chunks:
             row_copies[c].wait()
         if c >= 3:
             ratio = ratios(c - 3)
-        best = total = None
-        for k in range(0, n_cent, tile):
-            if c == 0 and k + tile < n_cent:
-                centroids_tile(k + tile)
-            if c < n_chunks:
-                m = logits_tile(c, k)
-                best = m if best is None else jnp.maximum(best, m)
-            if c > 0:
-                part = exp_tile(c - 1, k, tops[c - 1])
-                total = part if total is None else total + part
-            if c >= 3:
-                weights_tile(c - 3, k, ratio)
+        best, total = [None, None], None
+        for k in range(0, n_cent, tall):
+            for j in range(2):
+                sub = k + j * tile
+                if c == 0 and sub + tall < n_cent:
+                    centroids_tile(sub + tall)
+                if c < n_chunks:
+                    m = logits_tile(c, k, j * wide_n)
+                    best[j] = m if best[j] is None else jnp.maximum(best[j], m)
+                if c > 0:
+                    part = exp_tile(c - 1, sub, tops[c - 1])
+                    total = part if total is None else total + part
+                if c >= 3:
+                    weights_tile(c - 3, sub, ratio)
         if c < n_chunks:
-            tops.append(jnp.max(best, axis=0, keepdims=True))
+            tops.append(jnp.max(jnp.concatenate(best, axis=1), axis=0, keepdims=True))
         if c == 1:
             pl.semaphore_wait(barrier, len(z_peers) + len(group))
         if c > 0:

time: 37.4 us -> 38.2 us (1.021)
  Pallas kernels: 35.9 us -> 36.7 us
    pallas_call x1, Pallas kernels: 33.9 us -> 34.6 us  [on_device(): pl.pallas_call(body, out_shape=(jax.ShapeDtypeStruct((n_cent, fb), f32),...]
where the time goes in v7:
time: 38.2 us; the launch traced here: 38 us
  Pallas kernels  36.7 us (96%)
  between operations  1.28 us (3%)
    pallas_call x1, Pallas kernels, on_device(): pl.pallas_call(body, out_shape=(jax.ShapeDtypeStruct((n_cent, fb), f32),...  34.6 us
    pallas_call x1, Pallas kernels, on_device(): pl.pallas_call(place, out_shape=(jax.ShapeDtypeStruct((fb, n_cent), f32),...  2.04 us

profile of v7, /device:TPU:0, one launch (start us, length us, event | category | flops | bytes accessed | tf_op | source)
XLA Modules:
  0.0 38.0 jit_solution(17122775043273938810)
XLA Ops:
  1.3 34.6 %shard_map.59 = (f32[1024,128]{1,0:T(8,128)}, f32[1,1024]{1,0:T(1,128)}) custom-call(bf16[2048,1024]{1,0:T(8,128)(2,1)} %rows_hbm.1, bf16[1024,1024]{1,0:T(8,128)(2,1)} %panel_hbm.1, f32[8,1024]{1,0:T(8,128)} %bitcast.2, s32[1]{0:T(128)S(6)} %copy.6.temp_ref), custom_call_target="tpu_custom_call" | custom-call | tf_op jit(solution)/shard_map/pallas_call | solution.py:292
  35.9 2.0 %shard_map.60 = (f32[128,1024]{1,0:T(8,128)}, f32[1,1024]{1,0:T(1,128)}) custom-call(f32[1024,128]{1,0:T(8,128)} %get-tuple-element.6.sums_ref, f32[1,1024]{1,0:T(1,128)} %get-tuple-element.7.counts_in), custom_call_target="tpu_custom_call" | custom-call | tf_op jit(solution)/shard_map/pallas_call | solution.py:325

commit v8 on v5

--- a/solution.py
+++ b/solution.py
@@ -243,14 +243,8 @@
 
     for i in range(1, dp_n):
         for h in range(2):
-            split(h, ranked[0][i], dot(0, n_rows, h, ranked[0][i]))
-            if first_step(ranked[0][i - 1], orders[h]) == 0:
-                finish(h, ranked[0][i - 1])
-    later = [(first_step(q, orders[h]), i, h, q) for h in range(2)
-             for i, q in enumerate(ranked[h]) if first_step(q, orders[h]) > 0]
-    later.sort()
-    for _, _, h, q in later[:-2]:
-        finish(h, q)
+            split(h, ranked[h][i], dot(0, n_rows, h, ranked[h][i]))
+            finish(h, ranked[h][i - 1])
 
     counts = cnt_out[...]
     for o, cp in enumerate(cnt_copies):
@@ -258,8 +252,8 @@
         counts = counts + cnt_in[o]
     counts_ref[...] = counts
 
-    for _, _, h, q in later[-2:]:
-        finish(h, q)
+    for h in range(2):
+        finish(h, ranked[h][-1])
 
     for cp in stat_copies + cnt_copies + list(core_copies.values()) + list(dp_copies.values()):
         cp.wait_send()

time: 37.4 us -> 35.2 us (0.941)
  Pallas kernels: 35.9 us -> 33.7 us
    pallas_call x1, Pallas kernels: 33.9 us -> 31.7 us  [on_device(): pl.pallas_call(body, out_shape=(jax.ShapeDtypeStruct((n_cent, fb), f32),...]
where the time goes in v8:
time: 35.2 us; the launch traced here: 35 us
  Pallas kernels  33.7 us (96%)
  between operations  1.28 us (4%)
    pallas_call x1, Pallas kernels, on_device(): pl.pallas_call(body, out_shape=(jax.ShapeDtypeStruct((n_cent, fb), f32),...  31.7 us
    pallas_call x1, Pallas kernels, on_device(): pl.pallas_call(place, out_shape=(jax.ShapeDtypeStruct((fb, n_cent), f32),...  2.04 us

profile of v8, /device:TPU:0, one launch (start us, length us, event | category | flops | bytes accessed | tf_op | source)
XLA Modules:
  0.0 35.0 jit_solution(1227690620206924174)
XLA Ops:
  1.3 31.7 %shard_map.59 = (f32[1024,128]{1,0:T(8,128)}, f32[1,1024]{1,0:T(1,128)}) custom-call(bf16[2048,1024]{1,0:T(8,128)(2,1)} %rows_hbm.1, bf16[1024,1024]{1,0:T(8,128)(2,1)} %panel_hbm.1, f32[8,1024]{1,0:T(8,128)} %bitcast.2, s32[1]{0:T(128)S(6)} %copy.6.temp_ref), custom_call_target="tpu_custom_call" | custom-call | tf_op jit(solution)/shard_map/pallas_call | solution.py:280
  33.0 2.0 %shard_map.60 = (f32[128,1024]{1,0:T(8,128)}, f32[1,1024]{1,0:T(1,128)}) custom-call(f32[1024,128]{1,0:T(8,128)} %get-tuple-element.6.sums_ref, f32[1,1024]{1,0:T(1,128)} %get-tuple-element.7.counts_in), custom_call_target="tpu_custom_call" | custom-call | tf_op jit(solution)/shard_map/pallas_call | solution.py:313

commit v9 on v8

--- a/solution.py
+++ b/solution.py
@@ -243,8 +243,8 @@
 
     for i in range(1, dp_n):
         for h in range(2):
+            finish(h, ranked[h][i - 1])
             split(h, ranked[h][i], dot(0, n_rows, h, ranked[h][i]))
-            finish(h, ranked[h][i - 1])
 
     counts = cnt_out[...]
     for o, cp in enumerate(cnt_copies):

time: 35.2 us -> 35.1 us (level)
  no operation moved by 1% of the time
where the time goes in v9:
time: 35.1 us; the launch traced here: 34.8 us
  Pallas kernels  33.6 us (96%)
  between operations  1.28 us (4%)
    pallas_call x1, Pallas kernels, on_device(): pl.pallas_call(body, out_shape=(jax.ShapeDtypeStruct((n_cent, fb), f32),...  31.5 us
    pallas_call x1, Pallas kernels, on_device(): pl.pallas_call(place, out_shape=(jax.ShapeDtypeStruct((fb, n_cent), f32),...  2.04 us

profile of v9, /device:TPU:0, one launch (start us, length us, event | category | flops | bytes accessed | tf_op | source)
XLA Modules:
  0.0 34.8 jit_solution(9864907414851865299)
XLA Ops:
  1.3 31.5 %shard_map.59 = (f32[1024,128]{1,0:T(8,128)}, f32[1,1024]{1,0:T(1,128)}) custom-call(bf16[2048,1024]{1,0:T(8,128)(2,1)} %rows_hbm.1, bf16[1024,1024]{1,0:T(8,128)(2,1)} %panel_hbm.1, f32[8,1024]{1,0:T(8,128)} %bitcast.2, s32[1]{0:T(128)S(6)} %copy.6.temp_ref), custom_call_target="tpu_custom_call" | custom-call | tf_op jit(solution)/shard_map/pallas_call | solution.py:280
  32.8 2.0 %shard_map.60 = (f32[128,1024]{1,0:T(8,128)}, f32[1,1024]{1,0:T(1,128)}) custom-call(f32[1024,128]{1,0:T(8,128)} %get-tuple-element.6.sums_ref, f32[1,1024]{1,0:T(1,128)} %get-tuple-element.7.counts_in), custom_call_target="tpu_custom_call" | custom-call | tf_op jit(solution)/shard_map/pallas_call | solution.py:313
